TPU v7x, 512 devices: a whole 4x4x16 slice. The times are simulated.
512 devices in a mesh: vocab: 32 (over y, x, core), rows: 16 (over z).
Axes of the slice: x: 4, y: 4, z: 16, core: 2. Of those that a mesh axis runs over, the one named last changes fastest.
Arguments:
- h_student: bfloat16 [384, 2560], P('rows'), may hold values from -6 to 6, as said below
- h_teacher: bfloat16 [384, 5120], P('rows'), may hold values from -6 to 6, as said below
- w_student: bfloat16 [98304, 2560], P(('vocab', 'rows')), may hold values from -1 to 1, as said below
- w_teacher: bfloat16 [98304, 5120], P(('vocab', 'rows')), may hold values from -1 to 1, as said below
Outputs:
- losses: float32 [2, 384], P(None, 'rows')
- d_hidden: float32 [384, 2560], P('rows', 'vocab')
- d_weight: bfloat16 [98304, 2560], P(('vocab', 'rows'))
Inputs may be any that keep to these rules, and one draw needn't show every extreme that they name: `h_student`: real-valued hidden states. `h_teacher`: real-valued hidden states. `w_student`: real-valued embedding rows. `w_teacher`: real-valued embedding rows.
All inputs are finite; a program needn't handle non-finite values.
Results may differ from a plain program's by a relative error of at most 0.03.
Values may be sent and summed in bfloat16 or wider, within the bound.
No kernel may reach another device: no remote copies, remote signals or barrier semaphores. Data moves between devices by JAX's collectives and lax.ppermute only.
A program may use at most 64 MiB of HBM per device.

v0:
```python
import jax
import jax.numpy as jnp
from jax import lax
from jax.sharding import PartitionSpec as P

skew_mix = 0.1


def entry_logits(weight, hidden):
    return lax.dot_general(
        weight, hidden, (((1,), (1,)), ((), ())), preferred_element_type=jnp.float32
    )


def local(h_student, h_teacher, w_student, w_teacher):
    tok_rows = h_student.shape[0]
    student_all, teacher_all = (
        lax.all_gather(h_student, "rows", axis=0, tiled=True),
        lax.all_gather(h_teacher, "rows", axis=0, tiled=True),
    )
    student_logits = entry_logits(w_student, student_all)
    teacher_logits = entry_logits(w_teacher, teacher_all)
    student_top, teacher_top = lax.pmax(
        (jnp.max(student_logits, axis=0), jnp.max(teacher_logits, axis=0)), ("vocab", "rows")
    )
    student_total, teacher_total = lax.psum(
        (
            jnp.sum(jnp.exp(student_logits - student_top), axis=0),
            jnp.sum(jnp.exp(teacher_logits - teacher_top), axis=0),
        ),
        ("vocab", "rows"),
    )
    log_q = student_logits - student_top - jnp.log(student_total)
    log_p = teacher_logits - teacher_top - jnp.log(teacher_total)
    prob_q = jnp.exp(log_q)
    prob_p = jnp.exp(log_p)
    log_mix_fwd = jnp.logaddexp(jnp.log(skew_mix) + log_p, jnp.log(1.0 - skew_mix) + log_q)
    log_mix_rev = jnp.logaddexp(jnp.log(1.0 - skew_mix) + log_p, jnp.log(skew_mix) + log_q)
    grad_q = (
        -(1.0 - skew_mix) * jnp.exp(log_p - log_mix_fwd)
        + log_q
        - log_mix_rev
        - skew_mix * jnp.exp(log_q - log_mix_rev)
    )
    forward_kl, reverse_kl, inner = lax.psum(
        (
            jnp.sum(prob_p * (log_p - log_mix_fwd), axis=0),
            jnp.sum(prob_q * (log_q - log_mix_rev), axis=0),
            jnp.sum(prob_q * grad_q, axis=0),
        ),
        ("vocab", "rows"),
    )
    logit_grad = (prob_q * (grad_q - inner)).astype(jnp.bfloat16)
    d_weight = jnp.dot(logit_grad, student_all, preferred_element_type=jnp.float32).astype(
        jnp.bfloat16
    )
    whole_term = lax.dot_general(
        logit_grad, w_student, (((0,), (0,)), ((), ())), preferred_element_type=jnp.float32
    )
    feature_part = lax.psum_scatter(
        whole_term.astype(jnp.bfloat16), "vocab", scatter_dimension=1, tiled=True
    )
    d_hidden = lax.psum_scatter(feature_part, "rows", scatter_dimension=0, tiled=True).astype(
        jnp.float32
    )
    both_losses = jnp.stack([forward_kl, reverse_kl])
    losses = lax.dynamic_slice_in_dim(both_losses, lax.axis_index("rows") * tok_rows, tok_rows, 1)
    return (losses, d_hidden, d_weight)


def solution(mesh):
    return jax.shard_map(
        local,
        mesh=mesh,
        in_specs=(
            P("rows", None),
            P("rows", None),
            P(("vocab", "rows"), None),
            P(("vocab", "rows"), None),
        ),
        out_specs=(P(None, "rows"), P("rows", "vocab"), P(("vocab", "rows"), None)),
        check_vma=False,
    )
```

profile of v0, /device:TPU:6, one launch (start us, length us, event | category | flops | bytes accessed | tf_op | source)
XLA Modules:
  0.0 634.0 jit_solution(12413271000481701108)
XLA Ops:
  7.2 0.0 copy-start
  7.2 0.0 all-gather.5.cloned.1.call-start
  7.2 0.7 all-gather.5.cloned.1.call-update
  7.9 0.0 all-gather.3.cloned.1.call-start
  8.0 0.7 all-gather.3.cloned.1.call-update
  8.7 0.0 reduce-scatter.3.cloned.1.call-start
  8.7 79.0 %all-gather.5.cloned.1.call-done = bf16[384,2560]{1,0:T(8,128)(2,1)} async-done(((bf16[24,2560]{1,0:T(8,128)(2,1)}), bf16[384,2560]{1,0:T(8,128)(2,1)}) %all-gather.5.cloned.1.call-update) | async-done | bytes 1966096 | tf_op jit(solution)/shard_map/all_gather | solution.py:18
  87.7 2.7 fusion.3
  90.4 74.1 %all-gather.3.cloned.1.call-done = bf16[384,5120]{1,0:T(8,128)(2,1)} async-done(((bf16[24,5120]{1,0:T(8,128)(2,1)}), bf16[384,5120]{1,0:T(8,128)(2,1)}) %all-gather.3.cloned.1.call-update) | async-done | bytes 3932176 | tf_op jit(solution)/shard_map/all_gather | solution.py:19
  164.5 0.0 copy-done
  164.5 3.6 fusion.4
  168.1 0.0 copy-start.1
  168.1 101.1 %all-reduce.3 = (f32[384]{0:T(512)S(1)}, f32[384]{0:T(512)S(1)}) all-reduce(f32[384]{0:T(512)S(1)} %get-tuple-element.20, f32[384]{0:T(512)S(1)} %get-tuple-element.22), channel_id=1, replica_groups=mesh['vocab'=32,'rows'=16] {'vocab','rows'}, use_global_device_ids=true, to_apply=%region_5.0 | all-reduce | flops 768 | bytes 6144 | tf_op jit(solution)/shard_map/pmax | solution.py:23
  269.2 0.1 exponential_reduce_fusion
  269.3 99.4 %all-reduce.2 = (f32[384]{0:T(512)}, f32[384]{0:T(512)}) all-reduce(f32[384]{0:T(512)S(1)} %get-tuple-element.24, f32[384]{0:T(512)S(1)} %get-tuple-element.25), channel_id=1, replica_groups=mesh['vocab'=32,'rows'=16] {'vocab','rows'}, use_global_device_ids=true, to_apply=%region_7.0 | all-reduce | flops 768 | bytes 6144 | tf_op jit(solution)/shard_map/psum | solution.py:26
  368.7 0.7 log.7
  369.4 0.7 log.6
  370.1 1.9 multiply_reduce_fusion.1
  372.0 100.4 %all-reduce.1 = (f32[1,384]{1,0:T(1,128)S(1)}, f32[1,384]{1,0:T(1,128)S(1)}, f32[384]{0:T(512)S(1)}) all-reduce(f32[1,384]{1,0:T(1,128)S(1)} %stack.9, f32[1,384]{1,0:T(1,128)S(1)} %stack.10, f32[384]{0:T(512)} %get-tuple-element.11), channel_id=1, replica_groups=mesh['vocab'=32,'rows'=16] {'vocab','rows'}, use_global_device_ids=true, to_apply=%region_9.0 | all-reduce | flops 1152 | bytes 9216 | tf_op jit(solution)/shard_map/psum | solution.py:45
  472.4 1.0 multiply_convert_fusion
  473.4 0.0 copy-done.1
  473.5 2.2 convolution_convert_fusion
  475.7 0.0 reduce-scatter.3.cloned.1.call-update
  475.7 1.3 dynamic-slice
  477.6 0.6 fusion.2
  478.3 3.2 convolution_convert_fusion.1
  481.5 87.8 %reduce-scatter.3.cloned.1.call-done = bf16[384,80]{0,1:T(8,128)(2,1)} async-done(((bf16[384,2560]{0,1:T(8,128)(2,1)}), bf16[384,80]{0,1:T(8,128)(2,1)}) %reduce-scatter.3.cloned.1.call-update) | async-done | bytes 61456 | tf_op jit(solution)/shard_map/reduce_scatter | solution.py:60
  569.2 57.5 %all-reduce = bf16[384,80]{0,1:T(8,128)(2,1)S(1)} all-reduce(bf16[384,80]{0,1:T(8,128)(2,1)} %reduce-scatter.3.cloned.1.call-done), channel_id=3, replica_groups=mesh['vocab'=32,'rows'=16] {'rows'}, use_global_device_ids=true, to_apply=%region_15.0.clone | all-reduce | flops 30720 | bytes 122880
  626.7 0.1 dynamic-slice_convert_fusion
  626.8 0.7 copy.8
  (2 shorter events, 0.0 us)
Async XLA Ops:
  7.2 157.3 %copy-start = (bf16[192,5120]{1,0:T(8,128)(2,1)S(1)}, bf16[192,5120]{1,0:T(8,128)(2,1)}, u32[]{:S(2)}) copy-start(bf16[192,5120]{1,0:T(8,128)(2,1)} %param.7) | copy-start | bytes 5898244
  7.2 80.5 %all-gather.5.cloned.1.call-start = ((), (), s32[]{:S(2)}) async-start(), calls=%async_computation.2 | async-start | bytes 2088960 | tf_op jit(solution)/shard_map/all_gather | solution.py:18
  7.9 156.6 %all-gather.3.cloned.1.call-start = ((), (), s32[]{:S(2)}) async-start(), calls=%async_computation.1 | async-start | bytes 4177920 | tf_op jit(solution)/shard_map/all_gather | solution.py:19
  8.7 560.5 %reduce-scatter.3.cloned.1.call-start = ((), (), s32[]{:S(2)}) async-start(), calls=%async_computation.3 | async-start | bytes 2027520 | tf_op jit(solution)/shard_map/reduce_scatter | solution.py:60
  168.1 305.4 %copy-start.1 = (bf16[192,2560]{1,0:T(8,128)(2,1)S(1)}, bf16[192,2560]{1,0:T(8,128)(2,1)}, u32[]{:S(2)}) copy-start(bf16[192,2560]{1,0:T(8,128)(2,1)} %param.6) | copy-start | bytes 2949124
Sparse Core Ops, SparseCore 0:
  10.1 77.5 all-gather.4
  89.8 74.6 all-gather.2
  475.8 93.3 reduce-scatter.2
where the time goes:
time: 635 us; the launch traced here: 634 us
  blocking collectives  358 us (56%)
  waiting for transfers between devices  242 us (38%)
  between operations  14.4 us (2%)
  matrix products  11.7 us (2%)
    pmax x1, blocking collectives, local(): lax.pmax((jnp.max(student_logits, axis=0), jnp.max(teacher_logits, axis=0...  101 us
    psum x1, blocking collectives, local(): lax.psum((jnp.sum(prob_p * (log_p - log_mix_fwd), axis=0), jnp.sum(prob_q...  100 us
    psum x1, blocking collectives, local(): lax.psum((jnp.sum(jnp.exp(student_logits - student_top), axis=0), jnp.sum...  99.4 us
    reduce_scatter x1, waiting for transfers between devices, local(): lax.psum_scatter(whole_term.astype(jnp.bfloat16), 'vocab', scatter_dimens...  87.8 us
    all_gather x1, waiting for transfers between devices, local(): lax.all_gather(h_student, 'rows', axis=0, tiled=True)  79 us
    all_gather x1, waiting for transfers between devices, local(): lax.all_gather(h_teacher, 'rows', axis=0, tiled=True)  74.1 us
    unnamed x1, blocking collectives  57.5 us
  transfers between devices with their start and end apart: 3, of which 3 were waited for; matrix products, arithmetic and copies ran while one was open for 1% of the time, Pallas kernels for 0%

commit v1 on v0

v1 whole, which is shorter than its diff:
```python
import jax
import jax.numpy as jnp
from jax import lax
from jax.experimental import pallas as pl
from jax.experimental.pallas import tpu as pltpu
from jax.sharding import Mesh, PartitionSpec as P

skew_mix = 0.1
f32, bf16 = jnp.float32, jnp.bfloat16
PLANE = ("y", "x")
VOCAB = ("y", "x", "core")
EVERY = ("y", "x", "core", "rows")
NT = (((1,), (1,)), ((), ()))
NN = (((1,), (0,)), ((), ()))
MIB = 1024 * 1024


def params(mib=24, **kw):
    return pltpu.CompilerParams(vmem_limit_bytes=mib * MIB, **kw)


def cost(flops, nbytes, trans=0):
    return pl.CostEstimate(flops=flops, bytes_accessed=nbytes, transcendentals=trans)


def sds(shape, dtype):
    return jax.ShapeDtypeStruct(shape, dtype)


def lse(a, axis):
    top = jnp.max(a, axis=axis, keepdims=True)
    return top + jnp.log(jnp.sum(jnp.exp(a - top), axis=axis, keepdims=True))


def five(h_ref, w_ref):
    acc = None
    for k in range(5):
        part = lax.dot_general(
            w_ref[:, 256 * k : 256 * (k + 1)], h_ref[k], NT, preferred_element_type=f32
        )
        acc = part if acc is None else acc + part
    return acc


def half_kernel(core_ref, h_ref, ws_ref, wt_ref, out_ref):
    i = pl.program_id(0)

    @pl.when(i == 0)
    def _():
        out_ref[0] = five(h_ref, ws_ref)

    @pl.when(i == 1)
    def _():
        out_ref[1] = five(h_ref, wt_ref)

    @pl.when(i == 2)
    def _():
        out_ref[1] += five(h_ref, wt_ref)


def rest_kernel(core_ref, h_ref, ws_ref, wt_ref, part_ref, out_ref, lse_ref):
    i = pl.program_id(0)

    @pl.when(i == 0)
    def _():
        out_ref[0] = part_ref[0] + five(h_ref, ws_ref)

    @pl.when(i == 1)
    def _():
        out_ref[1] = part_ref[1] + five(h_ref, wt_ref)

    @pl.when(i == 2)
    def _():
        out_ref[1] += five(h_ref, wt_ref)
        both = jnp.concatenate([lse(out_ref[0], 0), lse(out_ref[1], 0)], axis=0)
        lse_ref[...] = jnp.broadcast_to(both[None], lse_ref.shape)


def logits_call(kernel, core, h, w_s, w_t, flip, part=None):
    ent, tok = w_s.shape[0], h.shape[1]
    in_specs = [
        pl.BlockSpec((5, tok, 256), lambda i, c: (i, 0, 0)),
        pl.BlockSpec((ent, 1280), lambda i, c: (0, c[0] ^ flip)),
        pl.BlockSpec((ent, 1280), lambda i, c: (0, 2 * (c[0] ^ flip) + jnp.maximum(i - 1, 0))),
    ]
    whole = pl.BlockSpec((2, ent, tok), lambda i, c: (0, 0, 0))
    out_shape, out_specs, args = [sds((2, ent, tok), f32)], [whole], [core, h, w_s, w_t]
    if part is not None:
        in_specs.append(whole)
        args.append(part)
        out_shape.append(sds((32, 2, tok), f32))
        out_specs.append(pl.BlockSpec((32, 2, tok), lambda i, c: (0, 0, 0)))
    return pl.pallas_call(
        kernel,
        grid_spec=pltpu.PrefetchScalarGridSpec(
            num_scalar_prefetch=1, grid=(3,), in_specs=in_specs, out_specs=out_specs
        ),
        out_shape=out_shape,
        compiler_params=params(),
        cost_estimate=cost(2 * ent * tok * 3840, 6_000_000, 150_000 if part is not None else 0),
    )(*args)


def merge_lse_kernel(a_ref, out_ref):
    out_ref[...] = jnp.broadcast_to(lse(a_ref[...], 0), out_ref.shape)


def minus_logaddexp(a, d):
    return -(jnp.maximum(a, d) + jnp.log1p(jnp.exp(-jnp.abs(a - d))))


def entries_kernel(norm_ref, logit_ref, qg_ref, sum_ref):
    norm = lse(norm_ref[...], 0)[0]
    log_q = logit_ref[0] - norm[0:1]
    log_p = logit_ref[1] - norm[1:2]
    d = log_p - log_q
    low, high = jnp.log(f32(skew_mix)), jnp.log(f32(1.0 - skew_mix))
    fwd = minus_logaddexp(low, high - d)
    rev = minus_logaddexp(high + d, low)
    q = jnp.exp(log_q)
    grad = -(1.0 - skew_mix) * jnp.exp(fwd) + rev - skew_mix * jnp.exp(rev)
    qg_ref[0] = q
    qg_ref[1] = grad
    sums = [
        jnp.sum(q * grad, axis=0, keepdims=True),
        jnp.sum(jnp.exp(log_p) * fwd, axis=0, keepdims=True),
        jnp.sum(q * rev, axis=0, keepdims=True),
    ]
    sum_ref[...] = jnp.broadcast_to(jnp.concatenate(sums, axis=0)[None], sum_ref.shape)


def merge_sum_kernel(a_ref, inner_ref, loss_ref):
    total = jnp.sum(a_ref[...], axis=0)
    inner_ref[...] = jnp.broadcast_to(total[None, 0:1], inner_ref.shape)
    loss_ref[...] = total[1:3]


def grad_kernel(inner_ref, own_ref, peer_ref, wt_own_ref, wt_peer_ref, lg_ref, dh_ref):
    inner = jnp.sum(inner_ref[...], axis=0)
    own = (own_ref[0] * (own_ref[1] - inner)).astype(bf16)
    peer = (peer_ref[0] * (peer_ref[1] - inner)).astype(bf16)
    lg_ref[...] = own
    for k in range(5):
        at = slice(256 * k, 256 * (k + 1))
        dh_ref[at, :] = (
            lax.dot_general(wt_own_ref[at, :], own, NN, preferred_element_type=f32)
            + lax.dot_general(wt_peer_ref[at, :], peer, NN, preferred_element_type=f32)
        ).astype(bf16)


def weight_kernel(core_ref, lg_ref, own_ref, peer_ref, out_ref):
    def fill(h_ref):
        for k in range(5):
            out_ref[:, 256 * k : 256 * (k + 1)] = lax.dot_general(
                lg_ref[...], h_ref[k], NN, preferred_element_type=f32
            ).astype(bf16)

    @pl.when(pl.program_id(0) == 0)
    def _():
        fill(own_ref)

    @pl.when(pl.program_id(0) == 1)
    def _():
        fill(peer_ref)


def plane_sum_kernel(a_ref, loss_ref, out_ref):
    total = jnp.sum(a_ref[...].astype(f32), axis=0)
    loss = loss_ref[...]
    high = loss.astype(bf16).astype(f32)
    mid = (loss - high).astype(bf16).astype(f32)
    rest = loss - high - mid
    pad = jnp.zeros((128 - total.shape[0] - 6, total.shape[1]), f32)
    out_ref[...] = jnp.concatenate([total, high, mid, rest, pad], axis=0).T.astype(bf16)


def rows_sum_kernel(a_ref, dh_ref, loss_ref):
    total = jnp.sum(a_ref[...].astype(f32), axis=0)
    cols, tok = dh_ref.shape[1], dh_ref.shape[0]
    dh_ref[...] = total[:, :cols]
    square = jnp.concatenate([total, jnp.zeros((128 - tok, 128), f32)], axis=0).T
    parts = square[cols : cols + 8]
    loss_ref[...] = (parts[0:2] + parts[2:4] + parts[4:6])[:, :tok]


def call(kernel, out_shape, *args, mib=24, flops=0, nbytes=1_000_000, trans=0):
    return pl.pallas_call(
        kernel,
        out_shape=out_shape,
        compiler_params=params(mib),
        cost_estimate=cost(flops, nbytes, trans),
    )(*args)


def copies(x, n):
    return jnp.broadcast_to(x[None], (n,) + x.shape)


def exchange(x, axes):
    return lax.all_to_all(x, axes, 0, 0)


def local(h_s, h_t, w_s, w_t):
    core = lax.axis_index("core")
    at = lax.axis_index(PLANE)
    core_arr = jnp.reshape(core, (1,)).astype(jnp.int32)
    swap = [(0, 1), (1, 0)]

    part_s = lax.dynamic_slice(h_s, (0, 1280 * core + 256 * jnp.minimum(at, 4)), (24, 256))
    part_t = lax.dynamic_slice(h_t, (0, 2560 * core + 256 * jnp.clip(at - 5, 0, 9)), (24, 256))
    piece = jnp.where(at < 5, part_s, part_t)
    tokens = exchange(copies(piece, 16), "rows").reshape(384, 256)
    own_h = exchange(copies(tokens, 16), PLANE)
    peer_h = lax.ppermute(own_h, "core", swap)

    by_core = w_s.reshape(192, 16, 2, 80).transpose(2, 1, 3, 0).reshape(2, 1280, 192)
    wt_own = lax.dynamic_index_in_dim(by_core, core, 0, keepdims=False)
    wt_peer = lax.ppermute(
        lax.dynamic_index_in_dim(by_core, 1 - core, 0, keepdims=False), "core", swap
    )

    (part,) = logits_call(half_kernel, core_arr, own_h, w_s, w_t, 0)
    logits, norm = logits_call(rest_kernel, core_arr, peer_h, w_s, w_t, 1, part)

    norm = call(merge_lse_kernel, sds((16, 2, 384), f32), exchange(norm, VOCAB))
    norm = exchange(norm, "rows")
    qg, sums = call(
        entries_kernel, [sds((2, 192, 384), f32), sds((32, 3, 384), f32)], norm, logits,
        nbytes=1_200_000, trans=600_000,
    )
    peer_qg = lax.ppermute(qg, "core", swap)
    inner, loss = call(
        merge_sum_kernel, [sds((16, 1, 384), f32), sds((2, 384), f32)], exchange(sums, VOCAB)
    )
    inner = exchange(inner, "rows")
    lg, dh = call(
        grad_kernel, [sds((192, 384), bf16), sds((1280, 384), bf16)],
        inner, qg, peer_qg, wt_own, wt_peer, flops=2 * 384 * 384 * 1280, nbytes=3_000_000,
    )
    d_weight = pl.pallas_call(
        weight_kernel,
        grid_spec=pltpu.PrefetchScalarGridSpec(
            num_scalar_prefetch=1,
            grid=(2,),
            in_specs=[
                pl.BlockSpec((192, 384), lambda i, c: (0, 0)),
                pl.BlockSpec((5, 384, 256), lambda i, c: (0, 0, 0)),
                pl.BlockSpec((5, 384, 256), lambda i, c: (0, 0, 0)),
            ],
            out_specs=pl.BlockSpec((192, 1280), lambda i, c: (0, c[0] ^ i)),
        ),
        out_shape=sds((192, 2560), bf16),
        compiler_params=params(),
        cost_estimate=cost(2 * 192 * 384 * 2560, 3_000_000),
    )(core_arr, lg, own_h, peer_h)

    dh = exchange(dh.reshape(16, 80, 384), PLANE)
    dh = call(plane_sum_kernel, sds((384, 128), bf16), dh, loss)
    dh = exchange(dh.reshape(16, 24, 128), "rows")
    d_hidden, losses = call(rows_sum_kernel, [sds((24, 80), f32), sds((2, 24), f32)], dh)
    return losses, d_hidden, d_weight


def solution(mesh):
    grid = Mesh(mesh.devices.reshape(4, 4, 2, 16), EVERY)
    return jax.shard_map(
        local,
        mesh=grid,
        in_specs=(P("rows", None), P("rows", None), P(EVERY, None), P(EVERY, None)),
        out_specs=(P(None, "rows"), P("rows", VOCAB), P(EVERY, None)),
        check_vma=False,
    )
```

time: 635 us -> 201 us (0.32)
  blocking collectives: 358 us -> 114 us
  waiting for transfers between devices: 242 us -> 31.6 us
  starting transfers between devices: 0.11 us -> 21.6 us
  local copies, waits for them, and re-layouts: 3.34 us -> 17.8 us
  between operations: 14.4 us -> 0.81 us
  matrix products: 11.7 us -> 0 us
  Pallas kernels: 0 us -> 11.5 us
    psum x2 -> x0, blocking collectives: 200 us -> none  [the longest x1 100 us: local(): lax.psum((jnp.sum(prob_p * (log_p - log_mix_fwd), axis=0), jnp.sum(prob_q...]
    all_gather x2 -> x0, waiting for transfers between devices: 153 us -> none  [the longest x1 79 us: local(): lax.all_gather(h_student, 'rows', axis=0, tiled=True)]
    all_to_all x0 -> x5, blocking collectives: none -> 114 us  [exchange(): return lax.all_to_all(x, axes, 0, 0)]
    pmax x1 -> x0, blocking collectives: 101 us -> none  [local(): lax.pmax((jnp.max(student_logits, axis=0), jnp.max(teacher_logits, axis=0...]
    reduce_scatter x1 -> x0, waiting for transfers between devices: 87.8 us -> none  [local(): lax.psum_scatter(whole_term.astype(jnp.bfloat16), 'vocab', scatter_dimens...]
    unnamed x1 -> x0, blocking collectives: 57.5 us -> none
    all_to_all x0 -> x3, waiting for transfers between devices: none -> 27.7 us  [exchange(): return lax.all_to_all(x, axes, 0, 0)]
    all_to_all x0 -> x3, starting transfers between devices: none -> 15.4 us  [exchange(): return lax.all_to_all(x, axes, 0, 0)]
  transfers between devices with their start and end apart: 3 -> 6, of which waited for: 3 -> 4; matrix products, arithmetic and copies ran while one was open for 1% -> 6% of each run, Pallas kernels for 0% -> 2%
where the time goes in v1:
time: 201 us; the launch traced here: 198 us
  blocking collectives  114 us (57%)
  waiting for transfers between devices  31.6 us (16%)
  starting transfers between devices  21.6 us (11%)
  local copies, waits for them, and re-layouts  17.8 us (9%)
  Pallas kernels  11.5 us (6%)
    all_to_all x5, blocking collectives, exchange(): return lax.all_to_all(x, axes, 0, 0)  114 us
    all_to_all x3, waiting for transfers between devices, exchange(): return lax.all_to_all(x, axes, 0, 0)  27.7 us
    all_to_all x3, starting transfers between devices, exchange(): return lax.all_to_all(x, axes, 0, 0)  15.4 us
    unnamed x17, local copies, waits for them, and re-layouts  8.34 us
    pallas_call x6, Pallas kernels, call(): pl.pallas_call(kernel, out_shape=out_shape, compiler_params=params(mib),...  6.45 us
    dynamic_slice x2, local copies, waits for them, and re-layouts, local(): lax.dynamic_index_in_dim(by_core, 1 - core, 0, keepdims=False)  4.54 us
  transfers between devices with their start and end apart: 6, of which 4 were waited for; matrix products, arithmetic and copies ran while one was open for 6% of the time, Pallas kernels for 2%

profile of v1, /device:TPU:6, one launch (start us, length us, event | category | flops | bytes accessed | tf_op | source)
XLA Modules:
  0.0 198.5 jit_solution(7949415561767796874)
XLA Ops:
  0.6 0.7 dynamic-slice_select_fusion
  1.4 31.4 %all_to_all.40 = bf16[16,24,256]{2,1,0:T(8,128)(2,1)S(1)} all-to-all(bf16[16,24,256]{2,1,0:T(8,128)(2,1)S(1)} %broadcast_in_dim.6), channel_id=1, replica_groups=mesh['y'=4,'x'=4,'core'=2,'rows'=16] {'rows'}, dimensions={0} | all-to-all | bytes 393216 | tf_op jit(solution)/shard_map/all_to_all | solution.py:200
  32.8 0.3 broadcast_in_dim.15
  33.1 0.0 copy-start.2
  33.1 0.0 copy-start.3
  33.2 41.3 %all_to_all.41.h_ref.own_ref = bf16[16,384,256]{2,1,0:T(8,128)(2,1)S(1)} all-to-all(bf16[16,384,256]{2,1,0:T(8,128)(2,1)S(1)} %broadcast_in_dim.15), channel_id=1, replica_groups=mesh['y'=4,'x'=4,'core'=2,'rows'=16] {'y','x'}, dimensions={0} | all-to-all | bytes 6291456 | tf_op jit(solution)/shard_map/all_to_all | solution.py:200
  74.5 1.9 collective-permute-start
  76.4 0.0 copy-done.2
  76.4 0.0 copy-done.3
  76.4 1.7 shard_map.67.part_ref
  78.1 3.9 %collective-permute-done.h_ref.peer_ref = bf16[16,384,256]{2,1,0:T(8,128)(2,1)S(1)} collective-permute-done((bf16[16,384,256]{2,1,0:T(8,128)(2,1)S(1)}, bf16[16,384,256]{2,1,0:T(8,128)(2,1)S(1)}, u32[]{:S(2)}, u32[]{:S(2)}) %collective-permute-start) | collective-permute-done | bytes 3145760 | tf_op jit(solution)/shard_map/ppermute | solution.py:214
  82.0 0.0 copy-start
  82.0 1.8 shard_map.68
  83.8 0.0 copy-done
  83.8 0.0 copy-start.6
  83.8 0.8 copy-done.6
  84.6 11.9 %all_to_all.42.a_ref = f32[32,2,384]{2,1,0:T(2,128)S(1)} all-to-all(f32[32,2,384]{2,1,0:T(2,128)S(1)} %get-tuple-element.13), channel_id=1, replica_groups=mesh['y'=4,'x'=4,'core'=2,'rows'=16] {'y','x','core'}, dimensions={0} | all-to-all | bytes 196608 | tf_op jit(solution)/shard_map/all_to_all | solution.py:200
  96.5 0.7 shard_map.69
  97.2 7.7 %all-to-all-start.3 = ((f32[16,2,384]{2,1,0:T(2,128)}), f32[16,2,384]{2,1,0:T(2,128)S(1)}, u32[]{:S(2)}, u32[]{:S(2)}) async-start(f32[16,2,384]{2,1,0:T(2,128)} %shard_map.69), calls=%async_computation.3 | async-start | bytes 98304 | tf_op jit(solution)/shard_map/all_to_all | solution.py:200
  104.9 2.4 %copy.14 = bf16[192,2560]{0,1:T(8,128)(2,1)} copy(bf16[192,2560]{1,0:T(8,128)(2,1)} %ws_ref.3) | data formatting | bytes 1966080 | tf_op args[2]
  107.3 2.5 %copy.15 = bf16[2,16,80,192]{3,2,1,0:T(8,128)(2,1)} copy(bf16[2,16,80,192]{3,2,0,1:T(8,128)(2,1)} %bitcast.13) | data formatting | bytes 1966080 | tf_op jit(solution)/shard_map/transpose | solution.py:216
  109.8 7.8 %all-to-all-done.3.norm_ref = f32[16,2,384]{2,1,0:T(2,128)S(1)} async-done(((f32[16,2,384]{2,1,0:T(2,128)}), f32[16,2,384]{2,1,0:T(2,128)S(1)}, u32[]{:S(2)}, u32[]{:S(2)}) %all-to-all-start.3) | async-done | bytes 49184 | tf_op jit(solution)/shard_map/all_to_all | solution.py:200
  117.6 0.0 copy-start.7
  117.6 1.1 copy-done.7
  118.7 1.5 shard_map.70
  120.1 1.9 collective-permute-start.1
  122.0 2.5 %constant_dynamic-slice_fusion = (bf16[1,1280,192]{2,1,0:T(8,128)(2,1)}, bf16[1280,192]{1,0:T(8,128)(2,1)}) fusion(bf16[2,1280,192]{2,1,0:T(8,128)(2,1)} %bitcast.12, s32[]{:T(128)S(6)} %select_n.26, s32[]{:T(128)S(6)} %select_n.25), kind=kLoop, calls=%fused_computation.2 | loop fusion | bytes 1966088 | tf_op jit(solution)/shard_map/jit(dynamic_index_in_dim)/dynamic_slice | solution.py:219
  124.5 2.1 %copy.16 = bf16[1,1280,192]{1,2,0:T(8,128)(2,1)} copy(bf16[1,1280,192]{2,1,0:T(8,128)(2,1)} %get-tuple-element.23) | data formatting | bytes 983040 | tf_op jit(solution)/shard_map/jit(dynamic_index_in_dim)/dynamic_slice | solution.py:219
  126.6 2.4 %collective-permute-start.2 = (bf16[1280,192]{0,1:T(8,128)(2,1)}, bf16[1280,192]{0,1:T(8,128)(2,1)}, u32[]{:S(2)}, u32[]{:S(2)}) collective-permute-start(bf16[1280,192]{0,1:T(8,128)(2,1)} %bitcast.15), channel_id=1, source_target_pairs={{0,16},{16,0},{1,17},{17,1},{2,18},{18,2},{3,19},{19,3},{4,20},{20... | collective-permute-start | bytes 1474568 | tf_op jit(solution)/shard_map/ppermute | solution.py:218
  129.0 11.8 %all_to_all.43.a_ref = f32[32,3,384]{2,1,0:T(4,128)S(1)} all-to-all(f32[32,3,384]{2,1,0:T(4,128)S(1)} %get-tuple-element.15), channel_id=1, replica_groups=mesh['y'=4,'x'=4,'core'=2,'rows'=16] {'y','x','core'}, dimensions={0} | all-to-all | bytes 294912 | tf_op jit(solution)/shard_map/all_to_all | solution.py:200
  140.8 0.6 shard_map.71
  141.5 4.2 %all-to-all-start.5 = ((f32[16,1,384]{2,1,0:T(1,128)}), f32[16,1,384]{2,1,0:T(1,128)S(1)}, u32[]{:S(2)}, u32[]{:S(2)}) async-start(f32[16,1,384]{2,1,0:T(1,128)} %get-tuple-element.16), calls=%async_computation.5 | async-start | bytes 49152 | tf_op jit(solution)/shard_map/all_to_all | solution.py:200
  145.7 0.0 collective-permute-done.2
  145.7 2.1 %copy.17.wt_peer_ref = bf16[1280,192]{1,0:T(8,128)(2,1)} copy(bf16[1280,192]{0,1:T(8,128)(2,1)} %collective-permute-done.2) | data formatting | bytes 983040 | tf_op jit(solution)/shard_map/ppermute | solution.py:218
  147.8 10.5 %all-to-all-done.5.inner_ref = f32[16,1,384]{2,1,0:T(1,128)S(1)} async-done(((f32[16,1,384]{2,1,0:T(1,128)}), f32[16,1,384]{2,1,0:T(1,128)S(1)}, u32[]{:S(2)}, u32[]{:S(2)}) %all-to-all-start.5) | async-done | bytes 24608 | tf_op jit(solution)/shard_map/all_to_all | solution.py:200
  158.3 0.0 collective-permute-done.1.peer_ref
  158.3 0.0 copy-start.4
  158.3 1.1 copy-done.4
  159.3 0.0 copy-start.5
  159.3 1.1 copy-done.5
  160.4 2.1 %shard_map.72 = (bf16[192,384]{1,0:T(8,128)(2,1)S(1)}, bf16[1280,384]{1,0:T(8,128)(2,1)S(1)}) custom-call(f32[16,1,384]{2,1,0:T(1,128)S(1)} %all-to-all-done.5.inner_ref, f32[2,192,384]{2,1,0:T(8,128)} %get-tuple-element.17.own_ref, f32[2,192,384]{2,1,0:T(8,128)} %collective-permute-done.1.peer_ref, bf16[1280,192]{1,0:T(8,128)(2,1)S(1)} %copy-done.5, ...), custom_call_target="tpu_custom_call" | custom-call | flops 377487360 | bytes 3000000 | tf_op jit(solution)/shard_map/pallas_call | solution.py:187
  162.5 17.9 %all_to_all.44.a_ref = bf16[16,80,384]{2,1,0:T(8,128)(2,1)S(1)} all-to-all(bf16[16,80,384]{2,1,0:T(8,128)(2,1)S(1)} %bitcast.11), channel_id=1, replica_groups=mesh['y'=4,'x'=4,'core'=2,'rows'=16] {'y','x'}, dimensions={0} | all-to-all | bytes 1966080 | tf_op jit(solution)/shard_map/all_to_all | solution.py:200
  180.5 0.9 shard_map.73
  181.3 3.5 %all-to-all-start.7 = ((bf16[16,24,128]{2,1,0:T(8,128)(2,1)}), bf16[16,24,128]{2,1,0:T(8,128)(2,1)S(1)}, u32[]{:S(2)}, u32[]{:S(2)}) async-start(bf16[16,24,128]{2,1,0:T(8,128)(2,1)} %bitcast.8), calls=%async_computation.7 | async-start | bytes 196608 | tf_op jit(solution)/shard_map/all_to_all | solution.py:200
  184.8 0.0 copy-start.1
  184.8 1.9 copy-done.1
  186.7 1.6 shard_map.75
  188.4 9.4 %all-to-all-done.7.a_ref = bf16[16,24,128]{2,1,0:T(8,128)(2,1)S(1)} async-done(((bf16[16,24,128]{2,1,0:T(8,128)(2,1)}), bf16[16,24,128]{2,1,0:T(8,128)(2,1)S(1)}, u32[]{:S(2)}, u32[]{:S(2)}) %all-to-all-start.7) | async-done | bytes 98336 | tf_op jit(solution)/shard_map/all_to_all | solution.py:200
  197.8 0.7 shard_map.74
  (1 shorter events, 0.0 us)
Async XLA Ops:
  33.1 43.3 %copy-start.2 = (bf16[192,2560]{1,0:T(8,128)(2,1)S(1)}, bf16[192,2560]{1,0:T(8,128)(2,1)}, u32[]{:S(2)}) copy-start(bf16[192,2560]{1,0:T(8,128)(2,1)} %ws_ref.3) | copy-start | bytes 2949124
  33.1 43.3 %copy-start.3 = (bf16[192,5120]{1,0:T(8,128)(2,1)S(1)}, bf16[192,5120]{1,0:T(8,128)(2,1)}, u32[]{:S(2)}) copy-start(bf16[192,5120]{1,0:T(8,128)(2,1)} %wt_ref.3) | copy-start | bytes 5898244
  74.5 7.5 %collective-permute-start = (bf16[16,384,256]{2,1,0:T(8,128)(2,1)S(1)}, bf16[16,384,256]{2,1,0:T(8,128)(2,1)S(1)}, u32[]{:S(2)}, u32[]{:S(2)}) collective-permute-start(bf16[16,384,256]{2,1,0:T(8,128)(2,1)S(1)} %all_to_all.41.h_ref.own_ref), channel_id=1, source_target_pairs={{0,16},{16,0},{1,17},{17,1},{2,18},{18,2},{3,19},{19,3},{4,20},{20... | collective-permute-start | bytes 9437192 | tf_op jit(solution)/shard_map/ppermute | solution.py:214
  82.0 1.8 copy-start
  83.8 0.8 copy-start.6
  97.2 20.4 %all-to-all-start.3 = ((f32[16,2,384]{2,1,0:T(2,128)}), f32[16,2,384]{2,1,0:T(2,128)S(1)}, u32[]{:S(2)}, u32[]{:S(2)}) async-start(f32[16,2,384]{2,1,0:T(2,128)} %shard_map.69), calls=%async_computation.3 | async-start | bytes 98304 | tf_op jit(solution)/shard_map/all_to_all | solution.py:200
  117.6 1.1 copy-start.7
  120.1 38.1 %collective-permute-start.1 = (f32[2,192,384]{2,1,0:T(8,128)}, f32[2,192,384]{2,1,0:T(8,128)}, u32[]{:S(2)}, u32[]{:S(2)}) collective-permute-start(f32[2,192,384]{2,1,0:T(8,128)} %get-tuple-element.17.own_ref), channel_id=1, source_target_pairs={{0,16},{16,0},{1,17},{17,1},{2,18},{18,2},{3,19},{19,3},{4,20},{20... | collective-permute-start | bytes 1769480 | tf_op jit(solution)/shard_map/ppermute | solution.py:231
  126.6 19.1 %collective-permute-start.2 = (bf16[1280,192]{0,1:T(8,128)(2,1)}, bf16[1280,192]{0,1:T(8,128)(2,1)}, u32[]{:S(2)}, u32[]{:S(2)}) collective-permute-start(bf16[1280,192]{0,1:T(8,128)(2,1)} %bitcast.15), channel_id=1, source_target_pairs={{0,16},{16,0},{1,17},{17,1},{2,18},{18,2},{3,19},{19,3},{4,20},{20... | collective-permute-start | bytes 1474568 | tf_op jit(solution)/shard_map/ppermute | solution.py:218
  141.5 16.8 %all-to-all-start.5 = ((f32[16,1,384]{2,1,0:T(1,128)}), f32[16,1,384]{2,1,0:T(1,128)S(1)}, u32[]{:S(2)}, u32[]{:S(2)}) async-start(f32[16,1,384]{2,1,0:T(1,128)} %get-tuple-element.16), calls=%async_computation.5 | async-start | bytes 49152 | tf_op jit(solution)/shard_map/all_to_all | solution.py:200
  158.3 1.1 copy-start.4
  159.3 1.1 copy-start.5
  181.3 16.5 %all-to-all-start.7 = ((bf16[16,24,128]{2,1,0:T(8,128)(2,1)}), bf16[16,24,128]{2,1,0:T(8,128)(2,1)S(1)}, u32[]{:S(2)}, u32[]{:S(2)}) async-start(bf16[16,24,128]{2,1,0:T(8,128)(2,1)} %bitcast.8), calls=%async_computation.7 | async-start | bytes 196608 | tf_op jit(solution)/shard_map/all_to_all | solution.py:200
  184.8 1.9 copy-start.1
